TPU v7x, 32 devices: a whole 2x2x4 slice. The times are simulated.
32 devices in a mesh: gx: 4 (over y, core), gy: 8 (over z, x).
Axes of the slice: x: 2, y: 2, z: 4, core: 2. Of those that a mesh axis runs over, the one named last changes fastest.
Arguments:
- state: float32 [286, 2, 16, 512], P(None, None, 'gy', 'gx'), may hold values from -6 to 6
- adjoint: float32 [286, 2, 16, 512], P(None, None, 'gy', 'gx'), may hold values from -6 to 6
- upwind_pos: float32 [3, 286, 286], replicated, may hold values from -0.375 to 0.375
- upwind_neg: float32 [3, 286, 286], replicated, may hold values from -0.375 to 0.375
- collision: float32 [35, 35, 35], replicated, may hold values from -0.15625 to 0.15625
- relax: float32 [286], replicated, may hold values from 0.1 to 2
- wall_table: float32 [3, 286], replicated, may hold values from 0 to 2
- drag_weights: float32 [286], replicated, may hold values from -6 to 6
- block_inverse: float32 [286, 286], replicated, may hold values from -0.375 to 0.375
- cell_codes: int32 [2, 16, 512], P(None, 'gy', 'gx'), may hold values from 0 to 3
- wall_mask: int32 [2, 16, 512], P(None, 'gy', 'gx'), may hold values 0 or 1
Outputs:
- state_next: float32 [286, 2, 16, 512], P(None, None, 'gy', 'gx')
- adjoint_next: float32 [286, 2, 16, 512], P(None, None, 'gy', 'gx')
All inputs are finite; a program needn't handle non-finite values. No bound on the sum of `wall_mask` on one device may be relied on, other than what follows from the above.
Results may differ from a plain program's by a relative error of at most 0.0003.
Values sent between devices are 32-bit elements; how exact they have to be, the bound alone decides.
A program may use at most 64 MiB of HBM per device.

v0:
```python
import jax
import jax.numpy as jnp
from jax import lax
from jax.sharding import PartitionSpec as P


def from_behind(block, axis, distance):
    devices = range(lax.axis_size(axis))
    route = [(i - distance, i) for i in devices if i - distance in devices]
    return lax.ppermute(block, axis, route)


def apply_matrix(matrix, field):
    return jnp.einsum("ab,bpyx->apyx", matrix, field, precision=lax.Precision.HIGHEST)


def apply_transposed(matrix, field):
    return jnp.einsum("ba,bpyx->apyx", matrix, field, precision=lax.Precision.HIGHEST)


def neighbours(center, received):
    x_prev, x_next, y_prev, y_next = received
    lanes = lax.broadcasted_iota(jnp.int32, center.shape, 3)
    rows = lax.broadcasted_iota(jnp.int32, center.shape, 2)
    last_lane = center.shape[3] - 1
    last_row = center.shape[2] - 1
    xminus = jnp.where(lanes == 0, x_prev, jnp.roll(center, 1, axis=3))
    xplus = jnp.where(lanes == last_lane, x_next, jnp.roll(center, -1, axis=3))
    yminus = jnp.where(rows == 0, y_prev, jnp.roll(center, 1, axis=2))
    yplus = jnp.where(rows == last_row, y_next, jnp.roll(center, -1, axis=2))
    zminus = jnp.roll(center, 1, axis=1)
    zplus = jnp.roll(center, -1, axis=1)
    return ((xminus, yminus, zminus), (xplus, yplus, zplus))


def on_device(
    state,
    adjoint,
    upwind_pos,
    upwind_neg,
    collision,
    relax,
    wall_table,
    drag_weights,
    block_inverse,
    cell_codes,
    wall_mask,
):
    state_recv = (
        from_behind(state[:, :, :, -1:], "gx", 1),
        from_behind(state[:, :, :, :1], "gx", -1),
        from_behind(state[:, :, -1:, :], "gy", 1),
        from_behind(state[:, :, :1, :], "gy", -1),
    )
    adjoint_recv = (
        from_behind(adjoint[:, :, :, -1:], "gx", 1),
        from_behind(adjoint[:, :, :, :1], "gx", -1),
        from_behind(adjoint[:, :, -1:, :], "gy", 1),
        from_behind(adjoint[:, :, :1, :], "gy", -1),
    )
    lowest = collision.shape[0]
    minus_all, plus_all = neighbours(state, state_recv)
    stream = jnp.zeros_like(state)
    for direction in range(3):
        stream = stream + apply_matrix(upwind_pos[direction], state - minus_all[direction])
        stream = stream + apply_matrix(upwind_neg[direction], plus_all[direction] - state)
    adminus, adplus = neighbours(adjoint, adjoint_recv)
    adstream = jnp.zeros_like(adjoint)
    for direction in range(3):
        adstream = adstream + apply_transposed(upwind_pos[direction], adjoint - adplus[direction])
        adstream = adstream + apply_transposed(upwind_neg[direction], adminus[direction] - adjoint)
    onehot = (cell_codes[None] == jnp.arange(1, 4, dtype=jnp.int32)[:, None, None, None]).astype(
        jnp.float32
    )
    damp = relax[:, None, None, None] + jnp.einsum(
        "cm,cpyx->mpyx", wall_table, onehot, precision=lax.Precision.HIGHEST
    )
    walls = wall_mask.astype(jnp.float32)[None]
    state_low = state[:lowest]
    adjoint_low = adjoint[:lowest]
    products = state_low[:, None] * state_low[None, :]
    gain = jnp.einsum("kab,abpyx->kpyx", collision, products, precision=lax.Precision.HIGHEST)
    symmetric = collision + jnp.transpose(collision, (0, 2, 1))
    cross = adjoint_low[:, None] * state_low[None, :]
    adgain = jnp.einsum("kij,kjpyx->ipyx", symmetric, cross, precision=lax.Precision.HIGHEST)
    primal_res = stream.at[:lowest].add(-gain) + damp * state
    state_next = state - 0.5 * apply_matrix(block_inverse, primal_res)
    adjoint_res = (
        adstream.at[:lowest].add(-adgain)
        + damp * adjoint
        - walls * drag_weights[:, None, None, None]
    )
    adjoint_next = adjoint - 0.5 * apply_transposed(block_inverse, adjoint_res)
    return (state_next, adjoint_next)


def solution(mesh):
    in_specs = (
        P(None, None, "gy", "gx"),
        P(None, None, "gy", "gx"),
        P(),
        P(),
        P(),
        P(),
        P(),
        P(),
        P(),
        P(None, "gy", "gx"),
        P(None, "gy", "gx"),
    )
    out_specs = (P(None, None, "gy", "gx"), P(None, None, "gy", "gx"))
    return jax.shard_map(
        on_device, mesh=mesh, in_specs=in_specs, out_specs=out_specs, check_vma=False
    )
```

profile of v0, /device:TPU:25, one launch (start us, length us, event | category | flops | bytes accessed | tf_op | source)
XLA Modules:
  0.0 88.6 jit_solution(10988368433318914969)
XLA Ops:
  0.6 0.0 copy-start
  0.6 0.0 copy-start.1
  0.7 2.1 %fusion.122 = (f32[286,2,2,1]{3,2,1,0:T(2,128)S(1)}, f32[286,2,2,1]{3,2,1,0:T(2,128)S(1)}) fusion(f32[286,2,2,128]{3,2,1,0:T(2,128)} %param.16), kind=kLoop, calls=%fused_computation.135 | loop fusion | bytes 18304 | tf_op jit(solution)/shard_map/slice | solution.py:56
  2.8 0.0 copy-start.2
  2.8 0.4 copy.149
  3.2 2.7 %collective-permute-start.4 = (f32[286,2,2,1]{0,2,3,1:T(2,128)S(1)}, f32[286,2,2,1]{0,2,3,1:T(2,128)S(1)}, u32[]{:S(2)}, u32[]{:S(2)}) collective-permute-start(f32[286,2,2,1]{0,2,3,1:T(2,128)S(1)} %copy.149), channel_id=1, source_target_pairs={{8,0},{16,8},{24,16},{9,1},{17,9},{25,17},{10,2},{18,10},{26,18},{... | collective-permute-start | bytes 13736 | tf_op jit(solution)/shard_map/ppermute | solution.py:10
  5.9 0.4 copy.150
  6.3 3.1 %collective-permute-start.5 = (f32[286,2,2,1]{0,2,3,1:T(2,128)S(1)}, f32[286,2,2,1]{0,2,3,1:T(2,128)S(1)}, u32[]{:S(2)}, u32[]{:S(2)}) collective-permute-start(f32[286,2,2,1]{0,2,3,1:T(2,128)S(1)} %copy.150), channel_id=1, source_target_pairs={{0,8},{8,16},{16,24},{1,9},{9,17},{17,25},{2,10},{10,18},{18,26},{... | collective-permute-start | bytes 13736 | tf_op jit(solution)/shard_map/ppermute | solution.py:10
  9.4 1.2 %fusion.121 = (f32[286,2,1,128]{3,2,1,0:T(1,128)}, f32[286,2,1,128]{3,2,1,0:T(1,128)S(1)}) fusion(f32[286,2,2,128]{3,2,1,0:T(2,128)S(1)} %copy-done.1), kind=kLoop, calls=%fused_computation.134 | loop fusion | bytes 1171456 | tf_op jit(solution)/shard_map/jit(_roll_static)/slice | solution.py:30
  10.6 3.0 %collective-permute-start.6 = (f32[286,2,1,128]{3,0,2,1:T(8,128)S(1)}, f32[286,2,1,128]{3,0,2,1:T(8,128)}, u32[]{:S(2)}, u32[]{:S(2)}) collective-permute-start(f32[286,2,1,128]{3,0,2,1:T(8,128)S(1)} %copy.195), channel_id=1, source_target_pairs={{1,0},{2,1},{3,2},{4,3},{5,4},{6,5},{7,6},{9,8},{10,9},{11,10},{12... | collective-permute-start | bytes 878600 | tf_op jit(solution)/shard_map/ppermute | solution.py:10
  13.6 0.8 fusion.127
  14.4 0.0 copy-start.9
  14.4 0.4 copy.147
  14.8 2.7 %collective-permute-start = (f32[286,2,2,1]{0,2,3,1:T(2,128)S(1)}, f32[286,2,2,1]{0,2,3,1:T(2,128)S(1)}, u32[]{:S(2)}, u32[]{:S(2)}) collective-permute-start(f32[286,2,2,1]{0,2,3,1:T(2,128)S(1)} %copy.147), channel_id=1, source_target_pairs={{0,8},{8,16},{16,24},{1,9},{9,17},{17,25},{2,10},{10,18},{18,26},{... | collective-permute-start | bytes 13736 | tf_op jit(solution)/shard_map/ppermute | solution.py:10
  17.5 0.4 copy.148
  17.8 1.9 %collective-permute-start.1 = (f32[286,2,2,1]{0,2,3,1:T(2,128)S(1)}, f32[286,2,2,1]{0,2,3,1:T(2,128)S(1)}, u32[]{:S(2)}, u32[]{:S(2)}) collective-permute-start(f32[286,2,2,1]{0,2,3,1:T(2,128)S(1)} %copy.148), channel_id=1, source_target_pairs={{8,0},{16,8},{24,16},{9,1},{17,9},{25,17},{10,2},{18,10},{26,18},{... | collective-permute-start | bytes 13736 | tf_op jit(solution)/shard_map/ppermute | solution.py:10
  19.8 1.8 %fusion.123 = (f32[286,2,2,127]{3,2,1,0:T(2,128)}, f32[286,2,2,127]{3,2,1,0:T(2,128)}) fusion(f32[286,2,2,128]{3,2,1,0:T(2,128)S(1)} %copy-done.1), kind=kLoop, calls=%fused_computation.136 | loop fusion | bytes 2324608 | tf_op jit(solution)/shard_map/jit(_roll_static)/slice | solution.py:27
  21.6 1.1 %fusion.120 = (f32[286,1,2,128]{3,2,1,0:T(2,128)}, f32[286,1,2,128]{3,2,1,0:T(2,128)}) fusion(f32[286,2,2,128]{3,2,1,0:T(2,128)S(1)} %copy-done.1), kind=kLoop, calls=%fused_computation.133 | loop fusion | bytes 1171456 | tf_op jit(solution)/shard_map/jit(_roll_static)/slice | solution.py:32
  22.7 1.8 %fusion.126 = (f32[286,2,2,127]{3,2,1,0:T(2,128)}, f32[286,2,2,127]{3,2,1,0:T(2,128)}) fusion(f32[286,2,2,128]{3,2,1,0:T(2,128)S(1)} %copy-done.2), kind=kLoop, calls=%fused_computation.139 | loop fusion | bytes 2324608 | tf_op jit(solution)/shard_map/jit(_roll_static)/slice | solution.py:28
  24.5 1.0 %fusion.124 = (f32[286,1,2,128]{3,2,1,0:T(2,128)}, f32[286,1,2,128]{3,2,1,0:T(2,128)}) fusion(f32[286,2,2,128]{3,2,1,0:T(2,128)S(1)} %copy-done.2), kind=kLoop, calls=%fused_computation.137 | loop fusion | bytes 1171456 | tf_op jit(solution)/shard_map/jit(_roll_static)/slice | solution.py:31
  25.6 1.3 %fusion.125 = (f32[286,2,1,128]{3,2,1,0:T(1,128)}, f32[286,2,1,128]{3,2,1,0:T(1,128)}) fusion(f32[286,2,2,128]{3,2,1,0:T(2,128)S(1)} %copy-done.2), kind=kLoop, calls=%fused_computation.138 | loop fusion | bytes 1171456 | tf_op jit(solution)/shard_map/slice | solution.py:52
  26.9 1.3 %fusion.14 = f32[286,2,2,128]{3,0,2,1:T(8,128)} fusion(f32[286]{0:T(512)S(1)} %copy-done.30, f32[3,286]{1,0:T(4,128)S(1)} %copy-done.29, s32[2,2,128]{2,1,0:T(2,128)S(1)} %copy-done.31, s32[3]{0:T(128)S(1)} %iota_add_fusion), kind=kOutput, calls=%fused_computation.27 | convolution fusion | flops 5419520 | bytes 592364 | tf_op jit(solution)/shard_map/cm,cpyx->mpyx/dot_general | solution.py:75
  28.2 0.7 copy.196
  29.0 1.2 %copy.112 = f32[35,35,35]{1,2,0:T(8,128)} copy(f32[35,35,35]{2,1,0:T(8,128)S(1)} %copy-done.13) | data formatting | bytes 343000 | tf_op args[4]
  30.2 1.7 %copy.194 = f32[286,2,1,128]{3,0,2,1:T(8,128)} copy(f32[286,2,1,128]{3,2,1,0:T(1,128)} %get-tuple-element.50) | data formatting | bytes 585728
  31.9 0.7 copy.193
  32.7 3.0 %collective-permute-start.7 = (f32[286,2,1,128]{3,0,2,1:T(8,128)}, f32[286,2,1,128]{3,0,2,1:T(8,128)}, u32[]{:S(2)}, u32[]{:S(2)}) collective-permute-start(f32[286,2,1,128]{3,0,2,1:T(8,128)} %copy.196), channel_id=1, source_target_pairs={{0,1},{1,2},{2,3},{3,4},{4,5},{5,6},{6,7},{8,9},{9,10},{10,11},{11... | collective-permute-start | bytes 878600 | tf_op jit(solution)/shard_map/ppermute | solution.py:10
  35.7 0.9 %copy.93 = f32[286,2,2]{2,1,0:T(2,128)} copy(f32[286,2,2]{0,2,1:T(2,128)S(1)} %bitcast.134) | data formatting | bytes 9152 | tf_op jit(solution)/shard_map/jit(_where)/broadcast_in_dim | solution.py:28
  36.6 1.9 %collective-permute-start.2 = (f32[286,2,1,128]{3,0,2,1:T(8,128)}, f32[286,2,1,128]{3,0,2,1:T(8,128)}, u32[]{:S(2)}, u32[]{:S(2)}) collective-permute-start(f32[286,2,1,128]{3,0,2,1:T(8,128)} %copy.194), channel_id=1, source_target_pairs={{0,1},{1,2},{2,3},{3,4},{4,5},{5,6},{6,7},{8,9},{9,10},{10,11},{11... | collective-permute-start | bytes 878600 | tf_op jit(solution)/shard_map/ppermute | solution.py:10
  38.5 0.9 %copy.98 = f32[286,2,2]{2,1,0:T(2,128)} copy(f32[286,2,2]{0,2,1:T(2,128)S(1)} %bitcast.133) | data formatting | bytes 9152 | tf_op jit(solution)/shard_map/jit(_where)/broadcast_in_dim | solution.py:27
  39.4 4.3 %collective-permute-start.3 = (f32[286,2,1,128]{3,0,2,1:T(8,128)}, f32[286,2,1,128]{3,0,2,1:T(8,128)}, u32[]{:S(2)}, u32[]{:S(2)}) collective-permute-start(f32[286,2,1,128]{3,0,2,1:T(8,128)} %copy.193), channel_id=1, source_target_pairs={{1,0},{2,1},{3,2},{4,3},{5,4},{6,5},{7,6},{9,8},{10,9},{11,10},{12... | collective-permute-start | bytes 878600 | tf_op jit(solution)/shard_map/ppermute | solution.py:10
  43.6 0.9 %copy.74 = f32[286,2,2]{2,1,0:T(2,128)} copy(f32[286,2,2]{0,2,1:T(2,128)S(1)} %bitcast.135) | data formatting | bytes 9152 | tf_op jit(solution)/shard_map/jit(_where)/broadcast_in_dim | solution.py:27
  44.6 0.9 %copy.78 = f32[286,2,2]{2,1,0:T(2,128)} copy(f32[286,2,2]{0,2,1:T(2,128)S(1)} %bitcast.136) | data formatting | bytes 9152 | tf_op jit(solution)/shard_map/jit(_where)/broadcast_in_dim | solution.py:28
  45.5 5.4 %fusion.102 = (f32[286,2,2,128]{3,2,1,0:T(2,128)S(1)}, f32[286,2,2,128]{3,2,1,0:T(2,128)S(1)}, f32[286,2,2,128]{3,2,1,0:T(2,128)S(1)}, f32[286,2,2,128]{3,2,1,0:T(2,128)S(1)}) fusion(f32[286,2,2,128]{3,2,1,0:T(2,128)S(1)} %copy-done.1, f32[286,1,2,128]{3,2,1,0:T(2,128)} %get-tuple-element.39, f32[286,1,2,128]{3,2,1,0:T(2,128)} %get-tuple-element.38, ...), kind=kLoop, calls=%fused_computation.110 | loop fusion | flops 1317888 | bytes 4695232 | tf_op jit(solution)/shard_map/sub | solution.py:71
  50.9 0.0 copy-start.5
  50.9 1.2 %fusion.41 = f32[2,2,128,286]{2,3,1,0:T(8,128)S(1)} fusion(f32[286,2,2,128]{3,2,1,0:T(2,128)S(1)} %get-tuple-element.37, f32[3,286,286]{2,1,0:T(8,128)S(1)} %copy-done.3), kind=kOutput, calls=%fused_computation.43 | convolution fusion | flops 502554624 | bytes 1613824 | tf_op jit(solution)/shard_map/ba,bpyx->apyx/dot_general | solution.py:18
  52.1 0.0 copy-start.10
  52.1 0.0 copy-start.21
  52.2 0.1 copy-done.5
  52.2 1.2 %convolution_add_fusion.4 = f32[2,2,128,286]{2,3,1,0:T(8,128)S(1)} fusion(f32[2,2,128,286]{2,3,1,0:T(8,128)S(1)} %fusion.41, f32[286,2,2,128]{3,2,1,0:T(2,128)S(1)} %get-tuple-element.36, f32[3,286,286]{2,1,0:T(8,128)S(1)} %copy-done.5), kind=kOutput, calls=%fused_computation.13 | convolution fusion | flops 502701056 | bytes 2203648 | tf_op jit(solution)/shard_map/ba,bpyx->apyx/dot_general | solution.py:18
  53.5 0.1 copy-done.21
  53.6 3.5 %fusion.104 = (f32[286,2,2,128]{3,2,1,0:T(2,128)}, f32[286,2,2,128]{3,2,1,0:T(2,128)}, f32[286,2,2,128]{3,2,1,0:T(2,128)S(1)}, f32[286,2,2,128]{3,2,1,0:T(2,128)S(1)}) fusion(f32[286,2,2,128]{3,2,1,0:T(2,128)S(1)} %copy-done.2, f32[286,1,2,128]{3,2,1,0:T(2,128)S(1)} %copy-done.24, f32[286,1,2,128]{3,2,1,0:T(2,128)S(1)} %copy-done.23, ...), kind=kLoop, calls=%fused_computation.112 | loop fusion | flops 1317888 | bytes 4695232 | tf_op jit(solution)/shard_map/sub | solution.py:66
  57.1 1.2 %fusion.46 = f32[2,2,128,286]{2,3,1,0:T(8,128)S(1)} fusion(f32[286,2,2,128]{3,2,1,0:T(2,128)S(1)} %get-tuple-element.47, f32[3,286,286]{2,1,0:T(8,128)S(1)} %copy-done.3), kind=kOutput, calls=%fused_computation.48 | convolution fusion | flops 502554624 | bytes 1613824 | tf_op jit(solution)/shard_map/ab,bpyx->apyx/dot_general | solution.py:14
  58.3 2.0 %convolution_add_fusion.9 = f32[2,2,128,286]{2,3,1,0:T(8,128)} fusion(f32[2,2,128,286]{2,3,1,0:T(8,128)S(1)} %fusion.46, f32[286,2,2,128]{3,2,1,0:T(2,128)S(1)} %get-tuple-element.46, f32[3,286,286]{2,1,0:T(8,128)S(1)} %copy-done.5), kind=kOutput, calls=%fused_computation.19 | convolution fusion | flops 502701056 | bytes 2203648 | tf_op jit(solution)/shard_map/ab,bpyx->apyx/dot_general | solution.py:14
  60.3 2.3 %convolution_add_fusion.3 = f32[2,2,128,286]{2,3,1,0:T(8,128)S(1)} fusion(f32[2,2,128,286]{2,3,1,0:T(8,128)S(1)} %convolution_add_fusion.4, f32[286,2,1,128]{3,0,2,1:T(8,128)S(1)} %copy.195, f32[286,2,1,128]{3,0,2,1:T(8,128)} %copy.196, f32[3,286,286]{2,1,0:T(8,128)S(1)} %copy-done.3, f32[286,2,128]{2,0,1:T(8,128)} %bitcast.37, ...), kind=kOutput, calls=%fused_computation.12 | convolution fusion | flops 503140352 | bytes 3084800 | tf_op jit(solution)/shard_map/ba,bpyx->apyx/dot_general | solution.py:18
  62.6 2.3 %convolution_add_fusion.2 = f32[2,2,128,286]{2,3,1,0:T(8,128)S(1)} fusion(f32[2,2,128,286]{2,3,1,0:T(8,128)S(1)} %convolution_add_fusion.3, f32[286,2,1,128]{3,0,2,1:T(8,128)S(1)} %copy.195, f32[286,2,1,128]{3,0,2,1:T(8,128)} %copy.196, f32[3,286,286]{2,1,0:T(8,128)S(1)} %copy-done.5, f32[286,2,128]{2,0,1:T(8,128)} %bitcast.39, ...), kind=kOutput, calls=%fused_computation.11 | convolution fusion | flops 503140352 | bytes 3084800 | tf_op jit(solution)/shard_map/ba,bpyx->apyx/dot_general | solution.py:18
  65.0 1.2 %convolution_add_fusion.1 = f32[2,2,128,286]{2,3,1,0:T(8,128)S(1)} fusion(f32[2,2,128,286]{2,3,1,0:T(8,128)S(1)} %convolution_add_fusion.2, f32[286,2,2,128]{3,2,1,0:T(2,128)S(1)} %get-tuple-element.33, f32[3,286,286]{2,1,0:T(8,128)S(1)} %copy-done.3), kind=kOutput, calls=%fused_computation.10 | convolution fusion | flops 502701056 | bytes 2203648 | tf_op jit(solution)/shard_map/ba,bpyx->apyx/dot_general | solution.py:18
  66.2 0.0 copy-start.14
  66.2 1.2 %fusion.11 = f32[286,2,2,128]{3,0,2,1:T(8,128)S(1)} fusion(f32[2,2,128,286]{2,3,1,0:T(8,128)S(1)} %convolution_add_fusion.1, f32[286,2,2,128]{3,2,1,0:T(2,128)S(1)} %get-tuple-element.32, f32[3,286,286]{2,1,0:T(8,128)S(1)} %copy-done.5), kind=kOutput, calls=%fused_computation.23 | convolution fusion | flops 502701056 | bytes 2203648 | tf_op jit(solution)/shard_map/ba,bpyx->apyx/dot_general | solution.py:18
  67.4 0.8 copy-done.17
  68.2 2.3 %fusion.33 = f32[35,2,2,128]{3,0,2,1:T(8,128)S(1)} fusion(f32[35,2,2,128]{3,0,2,1:T(8,128)S(1)} %copy.113, f32[35,2,2,128]{3,0,2,1:T(8,128)S(1)} %copy.87, f32[35,35,35]{2,1,0:T(8,128)S(1)} %copy-done.14, f32[35,35,35]{1,2,0:T(8,128)S(1)} %copy-done.16, f32[286,2,2,128]{3,0,2,1:T(8,128)S(1)} %fusion.11), kind=kOutput, calls=%fused_computation.34 | convolution fusion | flops 264129920 | bytes 629720 | tf_op jit(solution)/shard_map/kij,kjpyx->ipyx/dot_general | solution.py:85
  70.5 1.6 %scatter-add.9 = f32[286,2,2,128]{3,0,2,1:T(8,128)} dynamic-update-slice(f32[286,2,2,128]{3,0,2,1:T(8,128)} %copy-done.17, f32[35,2,2,128]{3,0,2,1:T(8,128)S(1)} %fusion.33, s32[]{:T(128)} %constant.51.clone.1, s32[]{:T(128)} %constant.51.clone.1, s32[]{:T(128)} %constant.51.clone.1, s32[]{:T(128)} %constant.51.clone.1) | dynamic-update-slice | bytes 143364 | tf_op jit(solution)/shard_map/scatter-add | solution.py:89
  72.2 2.6 %fusion.13 = f32[286,2,2,128]{3,0,2,1:T(8,128)S(1)} fusion(f32[286,2,2,128]{3,0,2,1:T(8,128)} %scatter-add.9, f32[286,2,2,128]{3,0,2,1:T(8,128)} %fusion.14, f32[286,286]{1,0:T(8,128)S(1)} %copy-done, f32[286]{0:T(512)S(1)} %copy-done.33, f32[2,2,128]{2,1,0:T(2,128)S(1)} %convert_element_type.4, f32[286,2,2,128]{3,2,1,0:T(2,128)S(1)} %copy-done.1), kind=kOutput, calls=%fused_computation.25 | convolution fusion | flops 503433216 | bytes 2673288 | tf_op jit(solution)/shard_map/ba,bpyx->apyx/dot_general | solution.py:18
  74.8 1.3 %copy.118 = f32[286,2,2,128]{3,2,1,0:T(2,128)} copy(f32[286,2,2,128]{3,0,2,1:T(8,128)S(1)} %fusion.13) | data formatting | bytes 1171456
  76.1 2.5 %convolution_add_fusion.8 = f32[2,2,128,286]{2,3,1,0:T(8,128)S(1)} fusion(f32[2,2,128,286]{2,3,1,0:T(8,128)S(1)} %copy-done.20, f32[286,2,1,128]{3,0,2,1:T(8,128)} %copy.193, f32[286,2,1,128]{3,0,2,1:T(8,128)} %copy.194, f32[3,286,286]{2,1,0:T(8,128)S(1)} %copy-done.3, f32[286,2,128]{2,0,1:T(8,128)} %bitcast.8, pred[2]{0:T(512)(128)(4,1)S(1)} %iota_compare_fusion.1, ...), kind=kOutput, calls=%fused_computation.18 | convolution fusion | flops 503140352 | bytes 3082752 | tf_op jit(solution)/shard_map/ab,bpyx->apyx/dot_general | solution.py:14
  78.6 2.4 %convolution_add_fusion.7 = f32[2,2,128,286]{2,3,1,0:T(8,128)S(1)} fusion(f32[2,2,128,286]{2,3,1,0:T(8,128)S(1)} %convolution_add_fusion.8, f32[286,2,1,128]{3,0,2,1:T(8,128)} %copy.193, f32[286,2,1,128]{3,0,2,1:T(8,128)} %copy.194, f32[3,286,286]{2,1,0:T(8,128)S(1)} %copy-done.6, f32[286,2,128]{2,0,1:T(8,128)} %bitcast.12, ...), kind=kOutput, calls=%fused_computation.17 | convolution fusion | flops 503140352 | bytes 3082752 | tf_op jit(solution)/shard_map/ab,bpyx->apyx/dot_general | solution.py:14
  81.1 0.0 copy-start.18
  81.1 1.2 %convolution_add_fusion.6 = f32[2,2,128,286]{2,3,1,0:T(8,128)S(1)} fusion(f32[2,2,128,286]{2,3,1,0:T(8,128)S(1)} %convolution_add_fusion.7, f32[286,2,2,128]{3,2,1,0:T(2,128)S(1)} %copy-done.19, f32[3,286,286]{2,1,0:T(8,128)S(1)} %copy-done.3), kind=kOutput, calls=%fused_computation.16 | convolution fusion | flops 502701056 | bytes 2203648 | tf_op jit(solution)/shard_map/ab,bpyx->apyx/dot_general | solution.py:14
  82.2 0.0 copy-start.15
  82.3 1.2 %fusion.8 = f32[286,2,2,128]{3,0,2,1:T(8,128)S(1)} fusion(f32[2,2,128,286]{2,3,1,0:T(8,128)S(1)} %convolution_add_fusion.6, f32[286,2,2,128]{3,2,1,0:T(2,128)S(1)} %copy-done.18, f32[3,286,286]{2,1,0:T(8,128)S(1)} %copy-done.6), kind=kOutput, calls=%fused_computation.20 | convolution fusion | flops 502701056 | bytes 2203648 | tf_op jit(solution)/shard_map/ab,bpyx->apyx/dot_general | solution.py:14
  83.5 2.4 %fusion.24 = f32[35,2,2,128]{3,0,2,1:T(8,128)S(1)} fusion(f32[35,2,2,128]{3,0,2,1:T(8,128)S(1)} %copy.87, f32[35,35,35,1,1]{2,1,0,4,3:T(8,128)S(1)} %bitcast.132, f32[286,2,2,128]{3,0,2,1:T(8,128)S(1)} %fusion.8), kind=kOutput, calls=%fused_computation.31 | convolution fusion | flops 264087040 | bytes 1034240 | tf_op jit(solution)/shard_map/kab,abpyx->kpyx/dot_general | solution.py:82
  85.8 0.3 scatter-add.6
  86.1 1.2 %fusion.10 = f32[286,2,2,128]{3,0,2,1:T(8,128)S(1)} fusion(f32[286,2,2,128]{3,0,2,1:T(8,128)S(1)} %scatter-add.6, f32[286,2,2,128]{3,0,2,1:T(8,128)S(1)} %copy-done.4, f32[286,286]{1,0:T(8,128)S(1)} %copy-done, f32[286,2,2,128]{3,2,1,0:T(2,128)S(1)} %copy-done.2), kind=kOutput, calls=%fused_computation.22 | convolution fusion | flops 503140352 | bytes 2670096 | tf_op jit(solution)/shard_map/ab,bpyx->apyx/dot_general | solution.py:14
  87.3 1.3 %copy.117 = f32[286,2,2,128]{3,2,1,0:T(2,128)} copy(f32[286,2,2,128]{3,0,2,1:T(8,128)S(1)} %fusion.10) | data formatting | bytes 1171456
  (75 shorter events, 0.2 us)
Async XLA Ops:
  0.6 71.5 %copy-start = (f32[286,286]{1,0:T(8,128)S(1)}, f32[286,286]{1,0:T(8,128)}, u32[]{:S(2)}) copy-start(f32[286,286]{1,0:T(8,128)} %param.23) | copy-start | bytes 981556
  0.6 8.7 %copy-start.1 = (f32[286,2,2,128]{3,2,1,0:T(2,128)S(1)}, f32[286,2,2,128]{3,2,1,0:T(2,128)}, u32[]{:S(2)}) copy-start(f32[286,2,2,128]{3,2,1,0:T(2,128)} %param.16) | copy-start | bytes 1757188
  2.8 7.8 %copy-start.7 = (f32[286,2,2,1]{3,2,1,0:T(2,128)}, f32[286,2,2,1]{3,2,1,0:T(2,128)S(1)}, u32[]{:S(2)}) copy-start(f32[286,2,2,1]{3,2,1,0:T(2,128)S(1)} %get-tuple-element.42) | copy-start | bytes 13732
  2.8 7.8 %copy-start.8 = (f32[286,2,2,1]{3,2,1,0:T(2,128)}, f32[286,2,2,1]{3,2,1,0:T(2,128)S(1)}, u32[]{:S(2)}) copy-start(f32[286,2,2,1]{3,2,1,0:T(2,128)S(1)} %get-tuple-element.43) | copy-start | bytes 13732
  2.8 10.8 %copy-start.2 = (f32[286,2,2,128]{3,2,1,0:T(2,128)S(1)}, f32[286,2,2,128]{3,2,1,0:T(2,128)}, u32[]{:S(2)}) copy-start(f32[286,2,2,128]{3,2,1,0:T(2,128)} %param.15) | copy-start | bytes 1757188
  3.2 29.5 %collective-permute-start.4 = (f32[286,2,2,1]{0,2,3,1:T(2,128)S(1)}, f32[286,2,2,1]{0,2,3,1:T(2,128)S(1)}, u32[]{:S(2)}, u32[]{:S(2)}) collective-permute-start(f32[286,2,2,1]{0,2,3,1:T(2,128)S(1)} %copy.149), channel_id=1, source_target_pairs={{8,0},{16,8},{24,16},{9,1},{17,9},{25,17},{10,2},{18,10},{26,18},{... | collective-permute-start | bytes 13736 | tf_op jit(solution)/shard_map/ppermute | solution.py:10
  6.3 30.3 %collective-permute-start.5 = (f32[286,2,2,1]{0,2,3,1:T(2,128)S(1)}, f32[286,2,2,1]{0,2,3,1:T(2,128)S(1)}, u32[]{:S(2)}, u32[]{:S(2)}) collective-permute-start(f32[286,2,2,1]{0,2,3,1:T(2,128)S(1)} %copy.150), channel_id=1, source_target_pairs={{0,8},{8,16},{16,24},{1,9},{9,17},{17,25},{2,10},{10,18},{18,26},{... | collective-permute-start | bytes 13736 | tf_op jit(solution)/shard_map/ppermute | solution.py:10
  10.6 49.7 %collective-permute-start.6 = (f32[286,2,1,128]{3,0,2,1:T(8,128)S(1)}, f32[286,2,1,128]{3,0,2,1:T(8,128)}, u32[]{:S(2)}, u32[]{:S(2)}) collective-permute-start(f32[286,2,1,128]{3,0,2,1:T(8,128)S(1)} %copy.195), channel_id=1, source_target_pairs={{1,0},{2,1},{3,2},{4,3},{5,4},{6,5},{7,6},{9,8},{10,9},{11,10},{12... | collective-permute-start | bytes 878600 | tf_op jit(solution)/shard_map/ppermute | solution.py:10
  14.4 7.3 %copy-start.9 = (f32[286,2,2,1]{3,2,1,0:T(2,128)}, f32[286,2,2,1]{3,2,1,0:T(2,128)S(1)}, u32[]{:S(2)}) copy-start(f32[286,2,2,1]{3,2,1,0:T(2,128)S(1)} %get-tuple-element.54) | copy-start | bytes 13732
  14.4 7.3 %copy-start.11 = (f32[286,2,2,1]{3,2,1,0:T(2,128)}, f32[286,2,2,1]{3,2,1,0:T(2,128)S(1)}, u32[]{:S(2)}) copy-start(f32[286,2,2,1]{3,2,1,0:T(2,128)S(1)} %get-tuple-element.55) | copy-start | bytes 13732
  14.8 24.6 %collective-permute-start = (f32[286,2,2,1]{0,2,3,1:T(2,128)S(1)}, f32[286,2,2,1]{0,2,3,1:T(2,128)S(1)}, u32[]{:S(2)}, u32[]{:S(2)}) collective-permute-start(f32[286,2,2,1]{0,2,3,1:T(2,128)S(1)} %copy.147), channel_id=1, source_target_pairs={{0,8},{8,16},{16,24},{1,9},{9,17},{17,25},{2,10},{10,18},{18,26},{... | collective-permute-start | bytes 13736 | tf_op jit(solution)/shard_map/ppermute | solution.py:10
  17.8 26.7 %collective-permute-start.1 = (f32[286,2,2,1]{0,2,3,1:T(2,128)S(1)}, f32[286,2,2,1]{0,2,3,1:T(2,128)S(1)}, u32[]{:S(2)}, u32[]{:S(2)}) collective-permute-start(f32[286,2,2,1]{0,2,3,1:T(2,128)S(1)} %copy.148), channel_id=1, source_target_pairs={{8,0},{16,8},{24,16},{9,1},{17,9},{25,17},{10,2},{18,10},{26,18},{... | collective-permute-start | bytes 13736 | tf_op jit(solution)/shard_map/ppermute | solution.py:10
  24.5 2.3 %copy-start.29 = (f32[3,286]{1,0:T(4,128)S(1)}, f32[3,286]{1,0:T(4,128)}, u32[]{:S(2)}) copy-start(f32[3,286]{1,0:T(4,128)} %param.21) | copy-start | bytes 10300
  24.5 2.3 %copy-start.30 = (f32[286]{0:T(512)S(1)}, f32[286]{0:T(512)}, u32[]{:S(2)}) copy-start(f32[286]{0:T(512)} %param.20) | copy-start | bytes 3436
  24.5 2.3 %copy-start.31 = (s32[2,2,128]{2,1,0:T(2,128)S(1)}, s32[2,2,128]{2,1,0:T(2,128)}, u32[]{:S(2)}) copy-start(s32[2,2,128]{2,1,0:T(2,128)} %param.24) | copy-start | bytes 6148
  24.5 3.7 %copy-start.27 = (f32[286,2,1,128]{3,2,1,0:T(1,128)S(1)}, f32[286,2,1,128]{3,2,1,0:T(1,128)}, u32[]{:S(2)}) copy-start(f32[286,2,1,128]{3,2,1,0:T(1,128)} %get-tuple-element.40) | copy-start | bytes 878596
  25.6 3.4 %slice-start.1 = ((f32[286,2,2,128]{3,2,1,0:T(2,128)}), f32[35,2,2,128]{3,2,1,0:T(2,128)S(1)}, s32[]{:S(2)}) async-start(f32[286,2,2,128]{3,2,1,0:T(2,128)} %param.15), calls=%async_computation.1 | async-start | bytes 143360 | tf_op jit(solution)/shard_map/slice | solution.py:79
  25.6 3.4 %copy-start.13 = (f32[35,35,35]{2,1,0:T(8,128)S(1)}, f32[35,35,35]{2,1,0:T(8,128)}, u32[]{:S(2)}) copy-start(f32[35,35,35]{2,1,0:T(8,128)} %param.19) | copy-start | bytes 514504
  28.2 2.0 %slice-start = ((f32[286,2,2,128]{3,2,1,0:T(2,128)}), f32[35,2,2,128]{3,2,1,0:T(2,128)S(1)}, s32[]{:S(2)}) async-start(f32[286,2,2,128]{3,2,1,0:T(2,128)} %param.16), calls=%async_computation | async-start | bytes 143360 | tf_op jit(solution)/shard_map/slice | solution.py:80
  28.2 2.0 %copy-start.32 = (s32[2,2,128]{2,1,0:T(2,128)S(1)}, s32[2,2,128]{2,1,0:T(2,128)}, u32[]{:S(2)}) copy-start(s32[2,2,128]{2,1,0:T(2,128)} %param.25) | copy-start | bytes 6148
  29.0 3.0 %copy-start.28 = (f32[286,2,1,128]{3,2,1,0:T(1,128)S(1)}, f32[286,2,1,128]{3,2,1,0:T(1,128)}, u32[]{:S(2)}) copy-start(f32[286,2,1,128]{3,2,1,0:T(1,128)} %get-tuple-element.51) | copy-start | bytes 878596
  32.7 30.0 %collective-permute-start.7 = (f32[286,2,1,128]{3,0,2,1:T(8,128)}, f32[286,2,1,128]{3,0,2,1:T(8,128)}, u32[]{:S(2)}, u32[]{:S(2)}) collective-permute-start(f32[286,2,1,128]{3,0,2,1:T(8,128)} %copy.196), channel_id=1, source_target_pairs={{0,1},{1,2},{2,3},{3,4},{4,5},{5,6},{6,7},{8,9},{9,10},{10,11},{11... | collective-permute-start | bytes 878600 | tf_op jit(solution)/shard_map/ppermute | solution.py:10
  36.6 39.5 %collective-permute-start.2 = (f32[286,2,1,128]{3,0,2,1:T(8,128)}, f32[286,2,1,128]{3,0,2,1:T(8,128)}, u32[]{:S(2)}, u32[]{:S(2)}) collective-permute-start(f32[286,2,1,128]{3,0,2,1:T(8,128)} %copy.194), channel_id=1, source_target_pairs={{0,1},{1,2},{2,3},{3,4},{4,5},{5,6},{6,7},{8,9},{9,10},{10,11},{11... | collective-permute-start | bytes 878600 | tf_op jit(solution)/shard_map/ppermute | solution.py:10
  39.4 39.2 %collective-permute-start.3 = (f32[286,2,1,128]{3,0,2,1:T(8,128)}, f32[286,2,1,128]{3,0,2,1:T(8,128)}, u32[]{:S(2)}, u32[]{:S(2)}) collective-permute-start(f32[286,2,1,128]{3,0,2,1:T(8,128)} %copy.193), channel_id=1, source_target_pairs={{1,0},{2,1},{3,2},{4,3},{5,4},{6,5},{7,6},{9,8},{10,9},{11,10},{12... | collective-permute-start | bytes 878600 | tf_op jit(solution)/shard_map/ppermute | solution.py:10
  45.5 5.4 %copy-start.3 = (f32[3,286,286]{2,1,0:T(8,128)S(1)}, f32[3,286,286]{2,1,0:T(8,128)}, u32[]{:S(2)}) copy-start(f32[3,286,286]{2,1,0:T(8,128)} %param.17) | copy-start | bytes 2944660
  45.5 7.9 %copy-start.23 = (f32[286,1,2,128]{3,2,1,0:T(2,128)S(1)}, f32[286,1,2,128]{3,2,1,0:T(2,128)}, u32[]{:S(2)}) copy-start(f32[286,1,2,128]{3,2,1,0:T(2,128)} %get-tuple-element.48) | copy-start | bytes 878596
  45.5 7.9 %copy-start.24 = (f32[286,1,2,128]{3,2,1,0:T(2,128)S(1)}, f32[286,1,2,128]{3,2,1,0:T(2,128)}, u32[]{:S(2)}) copy-start(f32[286,1,2,128]{3,2,1,0:T(2,128)} %get-tuple-element.49) | copy-start | bytes 878596
  45.5 7.9 %copy-start.25 = (f32[286,2,2]{2,1,0:T(2,128)S(1)}, f32[286,2,2]{2,1,0:T(2,128)}, u32[]{:S(2)}) copy-start(f32[286,2,2]{2,1,0:T(2,128)} %copy.74) | copy-start | bytes 13732
  45.5 7.9 %copy-start.26 = (f32[286,2,2]{2,1,0:T(2,128)S(1)}, f32[286,2,2]{2,1,0:T(2,128)}, u32[]{:S(2)}) copy-start(f32[286,2,2]{2,1,0:T(2,128)} %copy.78) | copy-start | bytes 13732
  50.9 1.3 %copy-start.5 = (f32[3,286,286]{2,1,0:T(8,128)S(1)}, f32[3,286,286]{2,1,0:T(8,128)}, u32[]{:S(2)}) copy-start(f32[3,286,286]{2,1,0:T(8,128)} %param.18) | copy-start | bytes 2944660
  50.9 2.5 %copy-start.22 = (f32[286,2,2,127]{3,2,1,0:T(2,128)S(1)}, f32[286,2,2,127]{3,2,1,0:T(2,128)}, u32[]{:S(2)}) copy-start(f32[286,2,2,127]{3,2,1,0:T(2,128)} %get-tuple-element.53) | copy-start | bytes 1743460
  52.1 1.3 %copy-start.10 = (f32[286,2,2,1]{3,2,1,0:T(2,128)S(1)}, f32[286,2,2,1]{3,2,1,0:T(2,128)}, u32[]{:S(2)}) copy-start(f32[286,2,2,1]{3,2,1,0:T(2,128)} %copy-done.9) | copy-start | bytes 13732
  52.1 1.3 %copy-start.12 = (f32[286,2,2,1]{3,2,1,0:T(2,128)S(1)}, f32[286,2,2,1]{3,2,1,0:T(2,128)}, u32[]{:S(2)}) copy-start(f32[286,2,2,1]{3,2,1,0:T(2,128)} %copy-done.11) | copy-start | bytes 13732
  52.1 1.4 %copy-start.21 = (f32[286,2,2,127]{3,2,1,0:T(2,128)S(1)}, f32[286,2,2,127]{3,2,1,0:T(2,128)}, u32[]{:S(2)}) copy-start(f32[286,2,2,127]{3,2,1,0:T(2,128)} %get-tuple-element.52) | copy-start | bytes 1743460
  66.2 2.0 %copy-start.14 = (f32[35,35,35]{2,1,0:T(8,128)S(1)}, f32[35,35,35]{2,1,0:T(8,128)}, u32[]{:S(2)}) copy-start(f32[35,35,35]{2,1,0:T(8,128)} %param.19) | copy-start | bytes 514504
  66.2 2.0 %copy-start.16 = (f32[35,35,35]{1,2,0:T(8,128)S(1)}, f32[35,35,35]{1,2,0:T(8,128)}, u32[]{:S(2)}) copy-start(f32[35,35,35]{1,2,0:T(8,128)} %copy.112) | copy-start | bytes 514504
  67.4 0.8 copy-start.17
  68.2 3.9 %copy-start.33 = (f32[286]{0:T(512)S(1)}, f32[286]{0:T(512)}, u32[]{:S(2)}) copy-start(f32[286]{0:T(512)} %param.22) | copy-start | bytes 3436
  72.2 3.9 %copy-start.20 = (f32[2,2,128,286]{2,3,1,0:T(8,128)S(1)}, f32[2,2,128,286]{2,3,1,0:T(8,128)}, u32[]{:S(2)}) copy-start(f32[2,2,128,286]{2,3,1,0:T(8,128)} %convolution_add_fusion.9) | copy-start | bytes 1757188
  76.1 2.5 %copy-start.6 = (f32[3,286,286]{2,1,0:T(8,128)S(1)}, f32[3,286,286]{2,1,0:T(8,128)}, u32[]{:S(2)}) copy-start(f32[3,286,286]{2,1,0:T(8,128)} %param.18) | copy-start | bytes 2944660
  78.6 2.5 %copy-start.19 = (f32[286,2,2,128]{3,2,1,0:T(2,128)S(1)}, f32[286,2,2,128]{3,2,1,0:T(2,128)}, u32[]{:S(2)}) copy-start(f32[286,2,2,128]{3,2,1,0:T(2,128)} %get-tuple-element.35) | copy-start | bytes 1757188
  81.1 1.2 %copy-start.18 = (f32[286,2,2,128]{3,2,1,0:T(2,128)S(1)}, f32[286,2,2,128]{3,2,1,0:T(2,128)}, u32[]{:S(2)}) copy-start(f32[286,2,2,128]{3,2,1,0:T(2,128)} %get-tuple-element.34) | copy-start | bytes 1757188
  82.2 1.2 %copy-start.15 = (f32[35,35,35]{2,1,0:T(8,128)S(1)}, f32[35,35,35]{2,1,0:T(8,128)}, u32[]{:S(2)}) copy-start(f32[35,35,35]{2,1,0:T(8,128)} %param.19) | copy-start | bytes 514504
  83.5 2.7 %copy-start.4 = (f32[286,2,2,128]{3,0,2,1:T(8,128)S(1)}, f32[286,2,2,128]{3,0,2,1:T(8,128)}, u32[]{:S(2)}) copy-start(f32[286,2,2,128]{3,0,2,1:T(8,128)} %fusion.14) | copy-start | bytes 1757188
where the time goes:
time: 90 us; the launch traced here: 88.6 us
  matrix products  29.6 us (33%)
  local copies, waits for them, and re-layouts  26.3 us (29%)
  starting transfers between devices  22.5 us (25%)
  other arithmetic  8.94 us (10%)
  between operations  1.24 us (1%)
    ppermute x8, starting transfers between devices, from_behind(): return lax.ppermute(block, axis, route)  22.5 us
    dot_general x7, matrix products, apply_transposed(): jnp.einsum('ba,bpyx->apyx', matrix, field, precision=lax.Precision.HIGHEST)  12 us
    dot_general x7, matrix products, apply_matrix(): jnp.einsum('ab,bpyx->apyx', matrix, field, precision=lax.Precision.HIGHEST)  11.6 us
    unnamed x79, local copies, waits for them, and re-layouts  9.59 us
    sub x1, other arithmetic, on_device(): adminus[direction] - adjoint  5.37 us
    sub x1, other arithmetic, on_device(): plus_all[direction] - state  3.55 us
    dot_general x1, matrix products, on_device(): jnp.einsum('kab,abpyx->kpyx', collision, products, precision=lax.Precisio...  2.35 us
    dot_general x1, matrix products, on_device(): jnp.einsum('kij,kjpyx->ipyx', symmetric, cross, precision=lax.Precision.H...  2.29 us
  transfers between devices with their start and end apart: 8, of which 0 were waited for; matrix products, arithmetic and copies ran while one was open for 58% of the time, Pallas kernels for 0%

commit v1 on v0

v1 whole, which is shorter than its diff:
```python
import functools
import jax
import jax.numpy as jnp
from jax import lax
from jax.experimental import pallas as pl
from jax.experimental.pallas import tpu as pltpu
from jax.sharding import PartitionSpec as P

F32 = jnp.float32
BF16 = jnp.bfloat16
MESH = pl.DeviceIdType.MESH

PX, NX, PY, NY, DZ, BI, HALO_PREV, HALO_NEXT = range(8)
N_SLOTS = 8


def split(x):
    high = x.astype(BF16)
    return high, (x - high.astype(F32)).astype(BF16)


def dot3(a_high, a_low, b_high, b_low):
    def dot(a, b):
        return jnp.dot(a, b, preferred_element_type=F32)

    return dot(a_high, b_high) + (dot(a_high, b_low) + dot(a_low, b_high))


def kernel(
    sizes,
    state, adjoint, pos, neg, coll, relax, table, drag, inverse, codes, walls,
    state_out, adjoint_out,
    lin, pos_v, neg_v, coll_v, relax_v, table_v, drag_v, inv_v, codes_v, walls_v,
    field, xsend, xrecv, halo, w_high, w_low, sym, zed, low, res, vecs, out_lin,
    in_sem, out_sem, xs_sem, xr_sem, ys_sem, yr_sem,
):
    moments, planes, rows, width, lowest, low_pad, n_gx, n_gy = sizes
    cells = planes * rows
    gx, gy = lax.axis_index("gx"), lax.axis_index("gy")
    has = {
        ("gx", 0): gx > 0, ("gx", 1): gx < n_gx - 1,
        ("gy", 0): gy > 0, ("gy", 1): gy < n_gy - 1,
    }
    where = {("gx", 0): gx - 1, ("gx", 1): gx + 1, ("gy", 0): gy - 1, ("gy", 1): gy + 1}

    loads = [
        pltpu.make_async_copy(src, dst, in_sem.at[i])
        for i, (src, dst) in enumerate(
            (
                (state, lin.at[0]), (adjoint, lin.at[1]), (coll, coll_v), (pos, pos_v),
                (neg, neg_v), (inverse, inv_v), (relax, relax_v), (table, table_v),
                (drag, drag_v), (codes, codes_v), (walls, walls_v),
            )
        )
    ]
    for load in loads:
        load.start()

    barrier = pltpu.get_barrier_semaphore()
    for side, there in has.items():
        @pl.when(there)
        def _(side=side):
            pl.semaphore_signal(
                barrier, inc=1, device_id={side[0]: where[side]}, device_id_type=MESH
            )
    pl.semaphore_wait(barrier, sum(there.astype(jnp.int32) for there in has.values()))

    def y_copy(f, to):
        return pltpu.make_async_remote_copy(
            src_ref=field.at[f, (rows - 1) * to],
            dst_ref=halo.at[f, 1 - to],
            send_sem=ys_sem.at[f, to],
            recv_sem=yr_sem.at[f, 1 - to],
            device_id={"gy": where["gy", to]},
            device_id_type=MESH,
        )

    def x_copy(to):
        return pltpu.make_async_remote_copy(
            src_ref=xsend.at[to],
            dst_ref=xrecv.at[1 - to],
            send_sem=xs_sem.at[to],
            recv_sem=xr_sem.at[1 - to],
            device_id={"gx": where["gx", to]},
            device_id_type=MESH,
        )

    for f in range(2):
        loads[f].wait()
        for p in range(planes):
            for y in range(rows):
                field[f, y, :, p * width:(p + 1) * width] = lin[
                    f, pl.ds(p * rows + y, moments, stride=cells), :
                ]
        for to in range(2):
            @pl.when(has["gy", to])
            def _(f=f, to=to):
                y_copy(f, to).start()

    lanes = lax.broadcasted_iota(jnp.int32, (moments, width), 1)
    firsts = jnp.zeros((moments, width), F32)
    lasts = jnp.zeros((moments, width), F32)
    for f in range(2):
        for p in range(planes):
            for y in range(rows):
                spot = f * cells + p * rows + y
                block = field[f, y, :, p * width:(p + 1) * width]
                firsts = jnp.where(lanes == spot, pltpu.roll(block, spot, 1), firsts)
                lasts = jnp.where(lanes == spot, pltpu.roll(block, spot + 1, 1), lasts)
    xsend[0] = firsts
    xsend[1] = lasts
    for to in range(2):
        @pl.when(has["gx", to])
        def _(to=to):
            x_copy(to).start()

        @pl.when(jnp.logical_not(has["gx", to]))
        def _(to=to):
            xrecv[to] = jnp.zeros((moments, width), F32)

        @pl.when(jnp.logical_not(has["gy", to]))
        def _(to=to):
            for f in range(2):
                halo[f, to] = jnp.zeros((moments, planes * width), F32)

    loads[2].wait()
    sym[...] = jnp.zeros(sym.shape, F32)
    for k in range(lowest):
        c = coll_v[k]
        sym[k * low_pad:k * low_pad + lowest, :] = 0.5 * (c + c.T)
    sym_high, sym_low = split(sym[...])
    for y in range(rows):
        s_low = field[0, y, :lowest, :]
        a_low = field[1, y, :lowest, :]
        zed[...] = dot3(sym_high, sym_low, *split(s_low))
        adgain = jnp.zeros(a_low.shape, F32)
        for k in range(lowest):
            z_k = zed[k * low_pad:k * low_pad + lowest, :]
            low[0, y, k:k + 1, :] = jnp.sum(z_k * s_low, axis=0, keepdims=True)
            adgain = adgain + z_k * a_low[k:k + 1, :]
        low[1, y, :lowest, :] = 2.0 * adgain

    for load in loads[3:]:
        load.wait()

    def keep(f, slot, matrix):
        high, rest = split(matrix)
        w_high[f, slot] = high
        w_low[f, slot] = rest

    for slot, matrix in (
        (PX, pos_v[0]), (NX, neg_v[0]), (PY, pos_v[1]), (NY, neg_v[1]),
        (DZ, pos_v[2] - neg_v[2]), (BI, inv_v[...]),
    ):
        keep(0, slot, matrix)
        keep(1, slot, matrix.T)

    def times(f, slot, x):
        return dot3(w_high[f, slot], w_low[f, slot], *split(x))

    def product(f, slot, scale):
        return scale * dot3(w_high[f, BI], w_low[f, BI], w_high[f, slot], w_low[f, slot])

    keep(0, HALO_PREV, product(0, PY, 0.5))
    keep(0, HALO_NEXT, product(0, NY, -0.5))
    keep(1, HALO_PREV, product(1, NY, -0.5))
    keep(1, HALO_NEXT, product(1, PY, 0.5))

    vecs[...] = jnp.zeros(vecs.shape, F32)
    vecs[0:3, :] = table_v[...]
    vecs[3:4, :] = relax_v[...].reshape(1, moments)
    vecs[4:5, :] = drag_v[...].reshape(1, moments)

    for to in range(2):
        @pl.when(has["gx", to])
        def _(to=to):
            x_copy(1 - to).wait_recv()

    edge = lax.broadcasted_iota(jnp.int32, (moments, width), 1)
    kinds = lax.broadcasted_iota(jnp.int32, (8, width), 0)

    def spread(table):
        return lax.dot_general(
            vecs[...], table, (((0,), (0,)), ((), ())),
            precision=lax.Precision.HIGHEST, preferred_element_type=F32,
        )

    for f in range(2):
        back, ahead = (PX, NX) if f == 0 else (NX, PX)
        y_back, y_ahead = (PY, NY) if f == 0 else (NY, PY)
        sign = 1.0 if f == 0 else -1.0
        z_diff = [field[f, y, :, :width] - field[f, y, :, width:] for y in range(rows)]
        z_part = times(f, DZ, jnp.concatenate(z_diff, axis=1))
        for y in range(rows):
            here = field[f, y]
            minus, plus, ones, marks = [], [], [], []
            for p in range(planes):
                spot = f * cells + p * rows + y
                block = here[:, p * width:(p + 1) * width]
                minus.append(jnp.where(
                    edge == 0, xrecv[0, :, spot:spot + 1], pltpu.roll(block, 1, 1)))
                plus.append(jnp.where(
                    edge == width - 1, xrecv[1, :, spot:spot + 1],
                    pltpu.roll(block, width - 1, 1)))
                code = codes_v[p, y:y + 1, :]
                ones.append(jnp.where(
                    kinds < 3, (code == kinds + 1).astype(F32), (kinds == 3).astype(F32)))
                wall = walls_v[p, y:y + 1, :].astype(F32)
                marks.append(jnp.where(kinds == 4, wall, 0.0))
            minus = jnp.concatenate(minus, axis=1)
            plus = jnp.concatenate(plus, axis=1)
            total = sign * (times(f, back, here - minus) + times(f, ahead, plus - here))
            y_minus = here - field[f, y - 1] if y > 0 else here
            y_plus = field[f, y + 1] - here if y < rows - 1 else -here
            total = total + sign * (times(f, y_back, y_minus) + times(f, y_ahead, y_plus))
            z_here = z_part[:, y * width:(y + 1) * width]
            total = total + jnp.concatenate([z_here, -z_here], axis=1)
            total = total + spread(jnp.concatenate(ones, axis=1)) * here
            if f == 1:
                total = total - spread(jnp.concatenate(marks, axis=1))
            res[...] = total
            res[:lowest, :] = res[:lowest, :] - low[f, y, :lowest, :]
            zed_out = here - 0.5 * times(f, BI, res[...])
            for p in range(planes):
                out_lin[f, pl.ds(p * rows + y, moments, stride=cells), :] = zed_out[
                    :, p * width:(p + 1) * width
                ]

    stores = []
    for f, target in enumerate((state_out, adjoint_out)):
        for side, y, slot in ((0, 0, HALO_PREV), (1, rows - 1, HALO_NEXT)):
            @pl.when(has["gy", side])
            def _(f=f, side=side):
                y_copy(f, 1 - side).wait_recv()

            late = times(f, slot, halo[f, side])
            for p in range(planes):
                spots = pl.ds(p * rows + y, moments, stride=cells)
                out_lin[f, spots, :] = out_lin[f, spots, :] + late[:, p * width:(p + 1) * width]
        store = pltpu.make_async_copy(out_lin.at[f], target, out_sem.at[f])
        store.start()
        stores.append(store)

    for to in range(2):
        @pl.when(has["gx", to])
        def _(to=to):
            x_copy(to).wait_send()

        @pl.when(has["gy", to])
        def _(to=to):
            for f in range(2):
                y_copy(f, to).wait_send()
    for store in stores:
        store.wait()


def on_device(
    n_gx, n_gy, state, adjoint, upwind_pos, upwind_neg, collision, relax, wall_table,
    drag_weights, block_inverse, cell_codes, wall_mask,
):
    moments, planes, rows, width = state.shape
    lowest = collision.shape[0]
    assert planes == 2 and 2 * planes * rows <= width
    low_pad = -(-lowest // 8) * 8
    flat = (moments * planes * rows, width)
    sizes = (moments, planes, rows, width, lowest, low_pad, n_gx, n_gy)
    out = jax.ShapeDtypeStruct(flat, F32)
    anywhere = pl.BlockSpec(memory_space=pl.ANY)
    outs = pl.pallas_call(
        functools.partial(kernel, sizes),
        out_shape=(out, out),
        in_specs=[pl.BlockSpec(memory_space=pltpu.HBM)] * 11,
        out_specs=(anywhere, anywhere),
        scratch_shapes=[
            pltpu.VMEM((2,) + flat, F32),
            pltpu.VMEM(upwind_pos.shape, F32),
            pltpu.VMEM(upwind_neg.shape, F32),
            pltpu.VMEM(collision.shape, F32),
            pltpu.VMEM(relax.shape, F32),
            pltpu.VMEM(wall_table.shape, F32),
            pltpu.VMEM(drag_weights.shape, F32),
            pltpu.VMEM(block_inverse.shape, F32),
            pltpu.VMEM(cell_codes.shape, jnp.int32),
            pltpu.VMEM(wall_mask.shape, jnp.int32),
            pltpu.VMEM((2, rows, moments, planes * width), F32),
            pltpu.VMEM((2, moments, width), F32),
            pltpu.VMEM((2, moments, width), F32),
            pltpu.VMEM((2, 2, moments, planes * width), F32),
            pltpu.VMEM((2, N_SLOTS, moments, moments), BF16),
            pltpu.VMEM((2, N_SLOTS, moments, moments), BF16),
            pltpu.VMEM((lowest * low_pad, lowest), F32),
            pltpu.VMEM((lowest * low_pad, planes * width), F32),
            pltpu.VMEM((2, rows, low_pad, planes * width), F32),
            pltpu.VMEM((moments, planes * width), F32),
            pltpu.VMEM((8, moments), F32),
            pltpu.VMEM((2,) + flat, F32),
            pltpu.SemaphoreType.DMA((11,)),
            pltpu.SemaphoreType.DMA((2,)),
            pltpu.SemaphoreType.DMA((2,)),
            pltpu.SemaphoreType.DMA((2,)),
            pltpu.SemaphoreType.DMA((2, 2)),
            pltpu.SemaphoreType.DMA((2, 2)),
        ],
        compiler_params=pltpu.CompilerParams(
            collective_id=0, has_side_effects=True, vmem_limit_bytes=52 * 1024 * 1024
        ),
    )(
        state.reshape(flat), adjoint.reshape(flat), upwind_pos, upwind_neg, collision, relax,
        wall_table, drag_weights, block_inverse, cell_codes, wall_mask,
    )
    return tuple(o.reshape(state.shape) for o in outs)


def solution(mesh):
    in_specs = (
        P(None, None, "gy", "gx"),
        P(None, None, "gy", "gx"),
        P(),
        P(),
        P(),
        P(),
        P(),
        P(),
        P(),
        P(None, "gy", "gx"),
        P(None, "gy", "gx"),
    )
    out_specs = (P(None, None, "gy", "gx"), P(None, None, "gy", "gx"))
    return jax.shard_map(
        functools.partial(on_device, mesh.shape["gx"], mesh.shape["gy"]),
        mesh=mesh, in_specs=in_specs, out_specs=out_specs, check_vma=False,
    )
```

time: 90 us -> 37.6 us (0.42); the launches traced: 88.6 us -> 37.2 us
  Pallas kernels: 0 us -> 30.5 us
  matrix products: 29.6 us -> 0 us
  starting transfers between devices: 22.5 us -> 0 us
  local copies, waits for them, and re-layouts: 26.3 us -> 6.05 us
  other arithmetic: 8.94 us -> 0 us
    pallas_call x0 -> x1, Pallas kernels: none -> 30.5 us  [on_device(): pl.pallas_call(functools.partial(kernel, sizes), out_shape=(out, out), in...]
    dot_general x17 -> x0, matrix products: 29.6 us -> none  [the longest x7 12 us: apply_transposed(): jnp.einsum('ba,bpyx->apyx', matrix, field, precision=lax.Precision.HIGHEST)]
    ppermute x8 -> x0, starting transfers between devices: 22.5 us -> none  [from_behind(): return lax.ppermute(block, axis, route)]
    slice x14 -> x0, local copies, waits for them, and re-layouts: 11.1 us -> none  [the longest x1 2.11 us: on_device(): adjoint[:, :, :, -1:]]
    sub x2 -> x0, other arithmetic: 8.92 us -> none  [the longest x1 5.37 us: on_device(): adminus[direction] - adjoint]
    broadcast_in_dim x4 -> x0, local copies, waits for them, and re-layouts: 3.64 us -> none  [the longest x2 1.83 us: neighbours(): xplus = jnp.where(lanes == last_lane, x_next, jnp.roll(center, -1, axis=3))]
    unnamed x79 -> x14, local copies, waits for them, and re-layouts: 9.59 us -> 6.05 us
    scatter-add x2 -> x0, local copies, waits for them, and re-layouts: 1.93 us -> none  [the longest x1 1.64 us: on_device(): adstream.at[:lowest].add(-adgain) + damp * adjoint]
  transfers between devices with their start and end apart: 8 -> 0, of which waited for: 0 -> 0; matrix products, arithmetic and copies ran while one was open for 58% -> 0% of each run, Pallas kernels for 0% -> 0%
where the time goes in v1:
time: 37.6 us; the launch traced here: 37.2 us
  Pallas kernels  30.5 us (81%)
  local copies, waits for them, and re-layouts  6.05 us (16%)
  between operations  0.66 us (2%)
    pallas_call x1, Pallas kernels, on_device(): pl.pallas_call(functools.partial(kernel, sizes), out_shape=(out, out), in...  30.5 us
    unnamed x14, local copies, waits for them, and re-layouts  6.05 us

profile of v1, /device:TPU:25, one launch (start us, length us, event | category | flops | bytes accessed | tf_op | source)
XLA Modules:
  0.0 37.2 jit_solution(462082895664131941)
XLA Ops:
  0.6 0.0 copy-start
  0.6 1.0 %copy-done = f32[286,286]{1,0:T(8,128)S(1)} copy-done((f32[286,286]{1,0:T(8,128)S(1)}, f32[286,286]{1,0:T(8,128)}, u32[]{:S(2)}) %copy-start) | copy-done | bytes 327208
  1.6 0.0 copy-start.1
  1.7 0.7 %copy-done.1 = f32[3,286]{1,0:T(4,128)S(1)} copy-done((f32[3,286]{1,0:T(4,128)S(1)}, f32[3,286]{1,0:T(4,128)}, u32[]{:S(2)}) %copy-start.1) | copy-done | bytes 3456
  2.3 0.0 copy-start.2
  2.3 0.7 %copy-done.2 = f32[286]{0:T(512)S(1)} copy-done((f32[286]{0:T(512)S(1)}, f32[286]{0:T(512)}, u32[]{:S(2)}) %copy-start.2) | copy-done | bytes 1168
  3.0 0.0 copy-start.3
  3.0 0.7 %copy-done.3 = f32[286]{0:T(512)S(1)} copy-done((f32[286]{0:T(512)S(1)}, f32[286]{0:T(512)}, u32[]{:S(2)}) %copy-start.3) | copy-done | bytes 1168
  3.7 0.0 copy-start.4
  3.7 0.7 %copy-done.4 = s32[2,2,128]{2,1,0:T(2,128)S(1)} copy-done((s32[2,2,128]{2,1,0:T(2,128)S(1)}, s32[2,2,128]{2,1,0:T(2,128)}, u32[]{:S(2)}) %copy-start.4) | copy-done | bytes 2072
  4.4 0.0 copy-start.5
  4.4 0.7 %copy-done.5 = s32[2,2,128]{2,1,0:T(2,128)S(1)} copy-done((s32[2,2,128]{2,1,0:T(2,128)S(1)}, s32[2,2,128]{2,1,0:T(2,128)}, u32[]{:S(2)}) %copy-start.5) | copy-done | bytes 2072
  5.1 30.5 %shard_map.122 = (f32[1144,128]{1,0:T(8,128)S(1)}, f32[1144,128]{1,0:T(8,128)S(1)}) custom-call(f32[1144,128]{1,0:T(8,128)} %bitcast.6, f32[1144,128]{1,0:T(8,128)} %bitcast.7, f32[3,286,286]{2,1,0:T(8,128)} %pos.1, f32[3,286,286]{2,1,0:T(8,128)} %neg.1, f32[35,35,35]{2,1,0:T(8,128)} %coll.1, f32[286]{0:T(512)S(1)} %copy-done.2, f32[3,286]{1,0:T(4,128)S(1)} %copy-done.1, ...), custom_call_target="tpu_custom_call" | custom-call | tf_op jit(solution)/shard_map/pallas_call | solution.py:269
  35.6 0.8 %copy.15 = f32[286,2,2,128]{3,2,1,0:T(2,128)} copy(f32[286,2,2,128]{3,2,1,0:T(2,128)S(1)} %bitcast.5) | data formatting | bytes 1171456
  36.4 0.8 %copy.16 = f32[286,2,2,128]{3,2,1,0:T(2,128)} copy(f32[286,2,2,128]{3,2,1,0:T(2,128)S(1)} %bitcast.4) | data formatting | bytes 1171456
Async XLA Ops:
  0.6 1.0 %copy-start = (f32[286,286]{1,0:T(8,128)S(1)}, f32[286,286]{1,0:T(8,128)}, u32[]{:S(2)}) copy-start(f32[286,286]{1,0:T(8,128)} %inverse.1) | copy-start | bytes 981556
  1.6 0.7 %copy-start.1 = (f32[3,286]{1,0:T(4,128)S(1)}, f32[3,286]{1,0:T(4,128)}, u32[]{:S(2)}) copy-start(f32[3,286]{1,0:T(4,128)} %table.1) | copy-start | bytes 10300
  2.3 0.7 %copy-start.2 = (f32[286]{0:T(512)S(1)}, f32[286]{0:T(512)}, u32[]{:S(2)}) copy-start(f32[286]{0:T(512)} %relax.1) | copy-start | bytes 3436
  3.0 0.7 %copy-start.3 = (f32[286]{0:T(512)S(1)}, f32[286]{0:T(512)}, u32[]{:S(2)}) copy-start(f32[286]{0:T(512)} %drag.1) | copy-start | bytes 3436
  3.7 0.7 %copy-start.4 = (s32[2,2,128]{2,1,0:T(2,128)S(1)}, s32[2,2,128]{2,1,0:T(2,128)}, u32[]{:S(2)}) copy-start(s32[2,2,128]{2,1,0:T(2,128)} %codes.1) | copy-start | bytes 6148
  4.4 0.7 %copy-start.5 = (s32[2,2,128]{2,1,0:T(2,128)S(1)}, s32[2,2,128]{2,1,0:T(2,128)}, u32[]{:S(2)}) copy-start(s32[2,2,128]{2,1,0:T(2,128)} %walls.1) | copy-start | bytes 6148

commit v2 on v1

v2 whole, which is shorter than its diff:
```python
import functools
import jax
import jax.numpy as jnp
from jax import lax
from jax.experimental import pallas as pl
from jax.experimental.pallas import tpu as pltpu
from jax.sharding import PartitionSpec as P

F32 = jnp.float32
BF16 = jnp.bfloat16
MESH = pl.DeviceIdType.MESH

PX, NX, PY, NY, DZ = range(5)
BLOCKS = 5
PIECES = 4
BI, HALO_PREV, HALO_NEXT = range(3)


def split(x):
    high = x.astype(BF16)
    return high, (x - high.astype(F32)).astype(BF16)


def dot(a, b):
    return jnp.dot(a, b, preferred_element_type=F32)


def dot3(a_high, a_low, b_high, b_low):
    return dot(a_high, b_high) + (dot(a_high, b_low) + dot(a_low, b_high))


def kernel(
    sizes,
    state, adjoint, pos, neg, coll, relax, table, drag, inverse, codes, walls,
    state_out, adjoint_out,
    lin, pos_v, neg_v, coll_v, relax_v, table_v, drag_v, inv_v, codes_v, walls_v,
    field, xsend, xrecv, halo, wide, wide_high, wide_low, tri, tri_b, rhs_high, rhs_low,
    sym, zed, low, res, vecs, out_lin,
    in_sem, out_sem, xs_sem, xr_sem, ys_sem, yr_sem,
):
    moments, planes, rows, width, lowest, low_pad, padded, n_gx, n_gy = sizes
    cells = planes * rows
    gx, gy = lax.axis_index("gx"), lax.axis_index("gy")
    has = {
        ("gx", 0): gx > 0, ("gx", 1): gx < n_gx - 1,
        ("gy", 0): gy > 0, ("gy", 1): gy < n_gy - 1,
    }
    where = {("gx", 0): gx - 1, ("gx", 1): gx + 1, ("gy", 0): gy - 1, ("gy", 1): gy + 1}

    loads = [
        pltpu.make_async_copy(src, dst, in_sem.at[i])
        for i, (src, dst) in enumerate(
            (
                (state, lin.at[0]), (adjoint, lin.at[1]), (coll, coll_v), (pos, pos_v),
                (neg, neg_v), (inverse, inv_v), (relax, relax_v), (table, table_v),
                (drag, drag_v), (codes, codes_v), (walls, walls_v),
            )
        )
    ]
    for load in loads:
        load.start()

    barrier = pltpu.get_barrier_semaphore()
    for side, there in has.items():
        @pl.when(there)
        def _(side=side):
            pl.semaphore_signal(
                barrier, inc=1, device_id={side[0]: where[side]}, device_id_type=MESH
            )
    field[:, :, moments:, :] = jnp.zeros((2, rows, padded - moments, planes * width), F32)
    pl.semaphore_wait(barrier, sum(there.astype(jnp.int32) for there in has.values()))

    def y_copy(f, to):
        return pltpu.make_async_remote_copy(
            src_ref=field.at[f, (rows - 1) * to],
            dst_ref=halo.at[f, 1 - to],
            send_sem=ys_sem.at[f, to],
            recv_sem=yr_sem.at[f, 1 - to],
            device_id={"gy": where["gy", to]},
            device_id_type=MESH,
        )

    def x_copy(to):
        return pltpu.make_async_remote_copy(
            src_ref=xsend.at[to],
            dst_ref=xrecv.at[1 - to],
            send_sem=xs_sem.at[to],
            recv_sem=xr_sem.at[1 - to],
            device_id={"gx": where["gx", to]},
            device_id_type=MESH,
        )

    for f in range(2):
        loads[f].wait()
        for p in range(planes):
            for y in range(rows):
                field[f, y, :moments, p * width:(p + 1) * width] = lin[
                    f, pl.ds(p * rows + y, moments, stride=cells), :
                ]
        for to in range(2):
            @pl.when(has["gy", to])
            def _(f=f, to=to):
                y_copy(f, to).start()

    lanes = lax.broadcasted_iota(jnp.int32, (padded, width), 1)
    firsts = jnp.zeros((padded, width), F32)
    lasts = jnp.zeros((padded, width), F32)
    for f in range(2):
        for p in range(planes):
            for y in range(rows):
                spot = f * cells + p * rows + y
                block = field[f, y, :, p * width:(p + 1) * width]
                firsts = jnp.where(lanes == spot, pltpu.roll(block, spot, 1), firsts)
                lasts = jnp.where(lanes == spot, pltpu.roll(block, spot + 1, 1), lasts)
    xsend[0] = firsts
    xsend[1] = lasts
    for to in range(2):
        @pl.when(has["gx", to])
        def _(to=to):
            x_copy(to).start()

        @pl.when(jnp.logical_not(has["gx", to]))
        def _(to=to):
            xrecv[to] = jnp.zeros((padded, width), F32)

        @pl.when(jnp.logical_not(has["gy", to]))
        def _(to=to):
            for f in range(2):
                halo[f, to] = jnp.zeros((padded, planes * width), F32)

    loads[2].wait()
    sym[...] = jnp.zeros(sym.shape, F32)
    for k in range(lowest):
        c = coll_v[k]
        sym[k * low_pad:k * low_pad + lowest, :lowest] = 0.5 * (c + c.T)
    half = sym.shape[1] // 2
    sym_all = sym[...]
    sym_top = sym_all.astype(BF16).astype(F32)
    sym_k = jnp.concatenate(
        [(sym_top + pltpu.roll(sym_top, half, 1)).astype(BF16), (sym_all - sym_top).astype(BF16)],
        axis=1,
    )
    for y in range(rows):
        s_low = field[0, y, :lowest, :]
        a_low = field[1, y, :lowest, :]
        s_pad = field[0, y, :half, :]
        keep_rows = lax.broadcasted_iota(jnp.int32, s_pad.shape, 0) < lowest
        s_high, s_rest = split(jnp.where(keep_rows, s_pad, 0.0))
        s_k = jnp.concatenate([s_high, s_rest, s_high, jnp.zeros_like(s_high)], axis=0)
        zed[...] = dot(sym_k, s_k)
        adgain = jnp.zeros(a_low.shape, F32)
        for k in range(lowest):
            z_k = zed[k * low_pad:k * low_pad + lowest, :]
            low[0, y, k:k + 1, :] = jnp.sum(z_k * s_low, axis=0, keepdims=True)
            adgain = adgain + z_k * a_low[k:k + 1, :]
        low[1, y, :lowest, :] = 2.0 * adgain

    for load in loads[3:]:
        load.wait()

    wide[...] = jnp.zeros(wide.shape, F32)
    tri[...] = jnp.zeros(tri.shape, F32)
    originals = (pos_v[0], neg_v[0], pos_v[1], neg_v[1], pos_v[2] - neg_v[2])

    def keep(f, slot, matrix):
        top = matrix.astype(BF16).astype(F32)
        tri[:moments, :moments] = top
        tri[:moments, padded:padded + moments] = top
        tri[:moments, 2 * padded:2 * padded + moments] = matrix - top
        tri_b[f, slot] = tri[...].astype(BF16)

    def times(f, slot, x):
        high, rest = split(x)
        return dot(tri_b[f, slot], jnp.concatenate([high, rest, high], axis=0))

    for f in range(2):
        for i, matrix in enumerate(originals):
            wide[:moments, i * padded:i * padded + moments] = matrix if f == 0 else matrix.T
        wide_high[f], wide_low[f] = split(wide[...])
        inv = inv_v[...] if f == 0 else inv_v[...].T
        inv_high, inv_low = split(inv)
        keep(f, BI, inv)
        for slot, block, scale in (
            (HALO_PREV, PY if f == 0 else NY, 0.5 if f == 0 else -0.5),
            (HALO_NEXT, NY if f == 0 else PY, -0.5 if f == 0 else 0.5),
        ):
            matrix = originals[block] if f == 0 else originals[block].T
            keep(f, slot, scale * dot3(inv_high, inv_low, *split(matrix)))

    vecs[...] = jnp.zeros(vecs.shape, F32)
    vecs[0:3, :moments] = table_v[...]
    vecs[3:4, :moments] = relax_v[...].reshape(1, moments)
    vecs[4:5, :moments] = drag_v[...].reshape(1, moments)
    whole = vecs[...]
    part1 = whole.astype(BF16).astype(F32)
    part2 = (whole - part1).astype(BF16).astype(F32)
    part3 = whole - part1 - part2
    parts = jnp.concatenate([part1, part2, part3], axis=0).T.astype(BF16)

    def spread(flags):
        return dot(parts, jnp.concatenate([flags] * 3, axis=0).astype(BF16))

    for to in range(2):
        @pl.when(has["gx", to])
        def _(to=to):
            x_copy(1 - to).wait_recv()

    kinds = lax.broadcasted_iota(jnp.int32, (8, width), 0)
    for y in range(rows):
        ones, marks = [], []
        for p in range(planes):
            code = codes_v[p, y:y + 1, :]
            ones.append(jnp.where(
                kinds < 3, (code == kinds + 1).astype(F32), (kinds == 3).astype(F32)))
            wall = walls_v[p, y:y + 1, :].astype(F32)
            marks.append(jnp.where(kinds == 4, wall, 0.0))
        damp = spread(jnp.concatenate(ones, axis=1))
        pull = spread(jnp.concatenate(marks, axis=1))
        for f in range(2):
            here = field[f, y]
            minus, plus = [], []
            for p in range(planes):
                spot = f * cells + p * rows + y
                block = here[:, p * width:(p + 1) * width]
                minus.append(jnp.where(
                    lanes == 0, xrecv[0, :, spot:spot + 1], pltpu.roll(block, 1, 1)))
                plus.append(jnp.where(
                    lanes == width - 1, xrecv[1, :, spot:spot + 1],
                    pltpu.roll(block, width - 1, 1)))
            x_minus = here - jnp.concatenate(minus, axis=1)
            x_plus = jnp.concatenate(plus, axis=1) - here
            y_minus = here - field[f, y - 1] if y > 0 else here
            y_plus = field[f, y + 1] - here if y < rows - 1 else -here
            z_diff = here[:, :width] - here[:, width:]
            z_both = jnp.concatenate([z_diff, -z_diff], axis=1)
            if f == 0:
                terms = (x_minus, x_plus, y_minus, y_plus, z_both)
            else:
                terms = (-x_plus, -x_minus, -y_plus, -y_minus, z_both)
            for i, term in enumerate(terms):
                rhs_high[i * padded:(i + 1) * padded, :], rhs_low[i * padded:(i + 1) * padded, :] = (
                    split(term)
                )
            total = dot3(wide_high[f], wide_low[f], rhs_high[...], rhs_low[...]) + damp * here
            if f == 1:
                total = total - pull
            res[...] = total
            res[:lowest, :] = res[:lowest, :] - low[f, y, :lowest, :]
            early = here - 0.5 * times(f, BI, res[...])
            for p in range(planes):
                out_lin[f, pl.ds(p * rows + y, moments, stride=cells), :] = early[
                    :moments, p * width:(p + 1) * width
                ]

    stores = []
    for f, target in enumerate((state_out, adjoint_out)):
        for side, y, slot in ((0, 0, HALO_PREV), (1, rows - 1, HALO_NEXT)):
            @pl.when(has["gy", side])
            def _(f=f, side=side):
                y_copy(f, 1 - side).wait_recv()

            late = times(f, slot, halo[f, side])
            for p in range(planes):
                spots = pl.ds(p * rows + y, moments, stride=cells)
                out_lin[f, spots, :] = (
                    out_lin[f, spots, :] + late[:moments, p * width:(p + 1) * width]
                )
        store = pltpu.make_async_copy(out_lin.at[f], target, out_sem.at[f])
        store.start()
        stores.append(store)

    for to in range(2):
        @pl.when(has["gx", to])
        def _(to=to):
            x_copy(to).wait_send()

        @pl.when(has["gy", to])
        def _(to=to):
            for f in range(2):
                y_copy(f, to).wait_send()
    for store in stores:
        store.wait()


def hand_over(pieces, a, b, a_out, b_out, sems):
    copies = []
    for f, (src, dst) in enumerate(((a, a_out), (b, b_out))):
        for i, (start, size) in enumerate(pieces):
            spots = pl.ds(start, size)
            copies.append(pltpu.make_async_copy(src.at[spots], dst.at[spots], sems.at[f, i]))
    for copy in copies:
        copy.start()
    for copy in copies:
        copy.wait()


def on_device(
    n_gx, n_gy, state, adjoint, upwind_pos, upwind_neg, collision, relax, wall_table,
    drag_weights, block_inverse, cell_codes, wall_mask,
):
    moments, planes, rows, width = state.shape
    lowest = collision.shape[0]
    assert planes == 2 and 2 * planes * rows <= width and lowest <= 64
    low_pad = -(-lowest // 8) * 8
    padded = -(-moments // 32) * 32
    flat = (moments * planes * rows, width)
    sizes = (moments, planes, rows, width, lowest, low_pad, padded, n_gx, n_gy)
    out = jax.ShapeDtypeStruct(flat, F32)
    anywhere = pl.BlockSpec(memory_space=pl.ANY)
    outs = pl.pallas_call(
        functools.partial(kernel, sizes),
        out_shape=(out, out),
        in_specs=[pl.BlockSpec(memory_space=pltpu.HBM)] * 11,
        out_specs=(anywhere, anywhere),
        scratch_shapes=[
            pltpu.VMEM((2,) + flat, F32),
            pltpu.VMEM(upwind_pos.shape, F32),
            pltpu.VMEM(upwind_neg.shape, F32),
            pltpu.VMEM(collision.shape, F32),
            pltpu.VMEM(relax.shape, F32),
            pltpu.VMEM(wall_table.shape, F32),
            pltpu.VMEM(drag_weights.shape, F32),
            pltpu.VMEM(block_inverse.shape, F32),
            pltpu.VMEM(cell_codes.shape, jnp.int32),
            pltpu.VMEM(wall_mask.shape, jnp.int32),
            pltpu.VMEM((2, rows, padded, planes * width), F32),
            pltpu.VMEM((2, padded, width), F32),
            pltpu.VMEM((2, padded, width), F32),
            pltpu.VMEM((2, 2, padded, planes * width), F32),
            pltpu.VMEM((padded, BLOCKS * padded), F32),
            pltpu.VMEM((2, padded, BLOCKS * padded), BF16),
            pltpu.VMEM((2, padded, BLOCKS * padded), BF16),
            pltpu.VMEM((padded, 3 * padded), F32),
            pltpu.VMEM((2, 3, padded, 3 * padded), BF16),
            pltpu.VMEM((BLOCKS * padded, planes * width), BF16),
            pltpu.VMEM((BLOCKS * padded, planes * width), BF16),
            pltpu.VMEM((lowest * low_pad, 128), F32),
            pltpu.VMEM((lowest * low_pad, planes * width), F32),
            pltpu.VMEM((2, rows, low_pad, planes * width), F32),
            pltpu.VMEM((padded, planes * width), F32),
            pltpu.VMEM((8, padded), F32),
            pltpu.VMEM((2,) + flat, F32),
            pltpu.SemaphoreType.DMA((11,)),
            pltpu.SemaphoreType.DMA((2,)),
            pltpu.SemaphoreType.DMA((2,)),
            pltpu.SemaphoreType.DMA((2,)),
            pltpu.SemaphoreType.DMA((2, 2)),
            pltpu.SemaphoreType.DMA((2, 2)),
        ],
        compiler_params=pltpu.CompilerParams(
            collective_id=0, has_side_effects=True, vmem_limit_bytes=64 * 1024 * 1024
        ),
    )(
        state.reshape(flat), adjoint.reshape(flat), upwind_pos, upwind_neg, collision, relax,
        wall_table, drag_weights, block_inverse, cell_codes, wall_mask,
    )
    step = -(-flat[0] // (8 * PIECES)) * 8
    pieces = [(at, min(step, flat[0] - at)) for at in range(0, flat[0], step)]
    outs = pl.pallas_call(
        functools.partial(hand_over, pieces),
        out_shape=(out, out),
        in_specs=[anywhere] * 2,
        out_specs=(anywhere, anywhere),
        scratch_shapes=[pltpu.SemaphoreType.DMA((2, len(pieces)))],
        compiler_params=pltpu.CompilerParams(vmem_limit_bytes=64 * 1024 * 1024),
    )(*outs)
    return tuple(o.reshape(state.shape) for o in outs)


def solution(mesh):
    in_specs = (
        P(None, None, "gy", "gx"),
        P(None, None, "gy", "gx"),
        P(),
        P(),
        P(),
        P(),
        P(),
        P(),
        P(),
        P(None, "gy", "gx"),
        P(None, "gy", "gx"),
    )
    out_specs = (P(None, None, "gy", "gx"), P(None, None, "gy", "gx"))
    return jax.shard_map(
        functools.partial(on_device, mesh.shape["gx"], mesh.shape["gy"]),
        mesh=mesh, in_specs=in_specs, out_specs=out_specs, check_vma=False,
    )
```

time: 37.6 us -> 68.5 us (1.82)
  Pallas kernels: 30.5 us -> 67.7 us
  local copies, waits for them, and re-layouts: 6.05 us -> 0 us
    pallas_call x0 -> x1, Pallas kernels: none -> 36.7 us  [on_device(): pl.pallas_call(functools.partial(hand_over, pieces), out_shape=(out, out)...]
    unnamed x14 -> x0, local copies, waits for them, and re-layouts: 6.05 us -> none
where the time goes in v2:
time: 68.5 us; the launch traced here: 68.3 us
  Pallas kernels  67.7 us (99%)
    pallas_call x1, Pallas kernels, on_device(): pl.pallas_call(functools.partial(hand_over, pieces), out_shape=(out, out)...  36.7 us
    pallas_call x1, Pallas kernels, on_device(): pl.pallas_call(functools.partial(kernel, sizes), out_shape=(out, out), in...  31 us

profile of v2, /device:TPU:25, one launch (start us, length us, event | category | flops | bytes accessed | tf_op | source)
XLA Modules:
  0.0 68.3 jit_solution(2283454612776210890)
XLA Ops:
  0.6 31.0 %shard_map.122 = (f32[1144,128]{1,0:T(8,128)}, f32[1144,128]{1,0:T(8,128)}) custom-call(f32[1144,128]{1,0:T(8,128)} %bitcast.4, f32[1144,128]{1,0:T(8,128)} %bitcast.5, f32[3,286,286]{2,1,0:T(8,128)} %pos.1, f32[3,286,286]{2,1,0:T(8,128)} %neg.1, f32[35,35,35]{2,1,0:T(8,128)} %coll.1, f32[286]{0:T(512)} %relax.1, f32[3,286]{1,0:T(4,128)} %table.1, f32[286]{0:T(512)} %drag.1, ...), custom_call_target="tpu_custom_call" | custom-call | tf_op jit(solution)/shard_map/pallas_call | solution.py:310
  31.6 36.7 %shard_map.123 = (f32[1144,128]{1,0:T(8,128)}, f32[1144,128]{1,0:T(8,128)}) custom-call(f32[1144,128]{1,0:T(8,128)} %get-tuple-element.6.a, f32[1144,128]{1,0:T(8,128)} %get-tuple-element.7.b), custom_call_target="tpu_custom_call" | custom-call | tf_op jit(solution)/shard_map/pallas_call | solution.py:359

commit v3 on v2

--- a/solution.py
+++ b/solution.py
@@ -12,7 +12,7 @@
 
 PX, NX, PY, NY, DZ = range(5)
 BLOCKS = 5
-PIECES = 4
+PIECES = 2
 BI, HALO_PREV, HALO_NEXT = range(3)
 
 
@@ -90,6 +90,16 @@
             device_id_type=MESH,
         )
 
+    parity = lax.rem(gy, 2)
+
+    def send_rows(f, first):
+        for to in range(2):
+            turn = parity == to if first else parity != to
+
+            @pl.when(jnp.logical_and(has["gy", to], turn))
+            def _(to=to):
+                y_copy(f, to).start()
+
     for f in range(2):
         loads[f].wait()
         for p in range(planes):
@@ -97,10 +107,7 @@
                 field[f, y, :moments, p * width:(p + 1) * width] = lin[
                     f, pl.ds(p * rows + y, moments, stride=cells), :
                 ]
-        for to in range(2):
-            @pl.when(has["gy", to])
-            def _(f=f, to=to):
-                y_copy(f, to).start()
+        send_rows(f, True)
 
     lanes = lax.broadcasted_iota(jnp.int32, (padded, width), 1)
     firsts = jnp.zeros((padded, width), F32)
@@ -154,6 +161,9 @@
             low[0, y, k:k + 1, :] = jnp.sum(z_k * s_low, axis=0, keepdims=True)
             adgain = adgain + z_k * a_low[k:k + 1, :]
         low[1, y, :lowest, :] = 2.0 * adgain
+
+    for f in range(2):
+        send_rows(f, False)
 
     for load in loads[3:]:
         load.wait()
@@ -252,22 +262,33 @@
                     :moments, p * width:(p + 1) * width
                 ]
 
-    stores = []
-    for f, target in enumerate((state_out, adjoint_out)):
-        for side, y, slot in ((0, 0, HALO_PREV), (1, rows - 1, HALO_NEXT)):
-            @pl.when(has["gy", side])
-            def _(f=f, side=side):
-                y_copy(f, 1 - side).wait_recv()
-
-            late = times(f, slot, halo[f, side])
-            for p in range(planes):
-                spots = pl.ds(p * rows + y, moments, stride=cells)
-                out_lin[f, spots, :] = (
-                    out_lin[f, spots, :] + late[:moments, p * width:(p + 1) * width]
-                )
-        store = pltpu.make_async_copy(out_lin.at[f], target, out_sem.at[f])
-        store.start()
-        stores.append(store)
+    stores = [
+        pltpu.make_async_copy(out_lin.at[f], target, out_sem.at[f])
+        for f, target in enumerate((state_out, adjoint_out))
+    ]
+
+    def finish(f, side):
+        y, slot = ((0, HALO_PREV), (rows - 1, HALO_NEXT))[side]
+
+        @pl.when(has["gy", side])
+        def _():
+            y_copy(f, 1 - side).wait_recv()
+
+        late = times(f, slot, halo[f, side])
+        for p in range(planes):
+            spots = pl.ds(p * rows + y, moments, stride=cells)
+            out_lin[f, spots, :] = (
+                out_lin[f, spots, :] + late[:moments, p * width:(p + 1) * width]
+            )
+
+    for side in range(2):
+        @pl.when(parity == side)
+        def _(side=side):
+            for f in range(2):
+                finish(f, side)
+            for f in range(2):
+                finish(f, 1 - side)
+                stores[f].start()
 
     for to in range(2):
         @pl.when(has["gx", to])
@@ -282,15 +303,21 @@
         store.wait()
 
 
-def hand_over(pieces, a, b, a_out, b_out, sems):
-    copies = []
+def hand_over(pieces, a, b, a_out, b_out, held, in_sems, out_sems):
+    ins, outs = [], []
     for f, (src, dst) in enumerate(((a, a_out), (b, b_out))):
         for i, (start, size) in enumerate(pieces):
             spots = pl.ds(start, size)
-            copies.append(pltpu.make_async_copy(src.at[spots], dst.at[spots], sems.at[f, i]))
-    for copy in copies:
+            ins.append(pltpu.make_async_copy(
+                src.at[spots], held.at[f, spots], in_sems.at[f, i]))
+            outs.append(pltpu.make_async_copy(
+                held.at[f, spots], dst.at[spots], out_sems.at[f, i]))
+    for copy in ins:
         copy.start()
-    for copy in copies:
+    for arrived, leaving in zip(ins, outs):
+        arrived.wait()
+        leaving.start()
+    for copy in outs:
         copy.wait()
 
 
@@ -361,7 +388,11 @@
         out_shape=(out, out),
         in_specs=[anywhere] * 2,
         out_specs=(anywhere, anywhere),
-        scratch_shapes=[pltpu.SemaphoreType.DMA((2, len(pieces)))],
+        scratch_shapes=[
+            pltpu.VMEM((2,) + flat, F32),
+            pltpu.SemaphoreType.DMA((2, len(pieces))),
+            pltpu.SemaphoreType.DMA((2, len(pieces))),
+        ],
         compiler_params=pltpu.CompilerParams(vmem_limit_bytes=64 * 1024 * 1024),
     )(*outs)
     return tuple(o.reshape(state.shape) for o in outs)

time: 68.5 us -> 33.9 us (0.49)
  Pallas kernels: 67.7 us -> 33 us
    pallas_call x1, Pallas kernels: 36.7 us -> 2.03 us  [on_device(): pl.pallas_call(functools.partial(hand_over, pieces), out_shape=(out, out)...]
where the time goes in v3:
time: 33.9 us; the launch traced here: 33.6 us
  Pallas kernels  33 us (97%)
  between operations  0.64 us (2%)
    pallas_call x1, Pallas kernels, on_device(): pl.pallas_call(functools.partial(kernel, sizes), out_shape=(out, out), in...  31 us
    pallas_call x1, Pallas kernels, on_device(): pl.pallas_call(functools.partial(hand_over, pieces), out_shape=(out, out)...  2.03 us

profile of v3, /device:TPU:25, one launch (start us, length us, event | category | flops | bytes accessed | tf_op | source)
XLA Modules:
  0.0 33.6 jit_solution(1117419460917979111)
XLA Ops:
  0.6 31.0 %shard_map.122 = (f32[1144,128]{1,0:T(8,128)}, f32[1144,128]{1,0:T(8,128)}) custom-call(f32[1144,128]{1,0:T(8,128)} %bitcast.4, f32[1144,128]{1,0:T(8,128)} %bitcast.5, f32[3,286,286]{2,1,0:T(8,128)} %pos.1, f32[3,286,286]{2,1,0:T(8,128)} %neg.1, f32[35,35,35]{2,1,0:T(8,128)} %coll.1, f32[286]{0:T(512)} %relax.1, f32[3,286]{1,0:T(4,128)} %table.1, f32[286]{0:T(512)} %drag.1, ...), custom_call_target="tpu_custom_call" | custom-call | tf_op jit(solution)/shard_map/pallas_call | solution.py:337
  31.6 2.0 %shard_map.123 = (f32[1144,128]{1,0:T(8,128)}, f32[1144,128]{1,0:T(8,128)}) custom-call(f32[1144,128]{1,0:T(8,128)} %get-tuple-element.6.a, f32[1144,128]{1,0:T(8,128)} %get-tuple-element.7.b), custom_call_target="tpu_custom_call" | custom-call | tf_op jit(solution)/shard_map/pallas_call | solution.py:386

commit v4 on v3

--- a/solution.py
+++ b/solution.py
@@ -108,6 +108,9 @@
                     f, pl.ds(p * rows + y, moments, stride=cells), :
                 ]
         send_rows(f, True)
+
+    for f in range(2):
+        send_rows(f, False)
 
     lanes = lax.broadcasted_iota(jnp.int32, (padded, width), 1)
     firsts = jnp.zeros((padded, width), F32)
@@ -161,9 +164,6 @@
             low[0, y, k:k + 1, :] = jnp.sum(z_k * s_low, axis=0, keepdims=True)
             adgain = adgain + z_k * a_low[k:k + 1, :]
         low[1, y, :lowest, :] = 2.0 * adgain
-
-    for f in range(2):
-        send_rows(f, False)
 
     for load in loads[3:]:
         load.wait()

time: 33.9 us -> 33.8 us (level)
  no operation moved by 1% of the time
where the time goes in v4:
time: 33.8 us; the launch traced here: 33.7 us
  Pallas kernels  33 us (98%)
  between operations  0.64 us (2%)
    pallas_call x1, Pallas kernels, on_device(): pl.pallas_call(functools.partial(kernel, sizes), out_shape=(out, out), in...  31 us
    pallas_call x1, Pallas kernels, on_device(): pl.pallas_call(functools.partial(hand_over, pieces), out_shape=(out, out)...  2.03 us

profile of v4, /device:TPU:25, one launch (start us, length us, event | category | flops | bytes accessed | tf_op | source)
XLA Modules:
  0.0 33.7 jit_solution(4864593473882506167)
XLA Ops:
  0.6 31.0 %shard_map.122 = (f32[1144,128]{1,0:T(8,128)}, f32[1144,128]{1,0:T(8,128)}) custom-call(f32[1144,128]{1,0:T(8,128)} %bitcast.4, f32[1144,128]{1,0:T(8,128)} %bitcast.5, f32[3,286,286]{2,1,0:T(8,128)} %pos.1, f32[3,286,286]{2,1,0:T(8,128)} %neg.1, f32[35,35,35]{2,1,0:T(8,128)} %coll.1, f32[286]{0:T(512)} %relax.1, f32[3,286]{1,0:T(4,128)} %table.1, f32[286]{0:T(512)} %drag.1, ...), custom_call_target="tpu_custom_call" | custom-call | tf_op jit(solution)/shard_map/pallas_call | solution.py:337
  31.6 2.0 %shard_map.123 = (f32[1144,128]{1,0:T(8,128)}, f32[1144,128]{1,0:T(8,128)}) custom-call(f32[1144,128]{1,0:T(8,128)} %get-tuple-element.6.a, f32[1144,128]{1,0:T(8,128)} %get-tuple-element.7.b), custom_call_target="tpu_custom_call" | custom-call | tf_op jit(solution)/shard_map/pallas_call | solution.py:386
